TPU v7x, 512 devices: a whole 4x8x8 slice. The times are simulated.
512 devices in a mesh: gx: 32 (over y, x), gy: 4 (over z_lo), gz: 4 (over z_hi, core).
Axes of the slice: x: 4, y: 8, z: 8 (z_hi: 2, z_lo: 4; z = z_hi * 4 + z_lo), core: 2. Of those that a mesh axis runs over, the one named last changes fastest.
Arguments:
- volume: float32 [1024, 128, 1024], P('gx', 'gz', 'gy'), may hold values from -18 to 18, as said below
- start_block: float32 [1024, 256], replicated, may hold values from -6 to 6
Outputs:
- factor: float32 [1024, 256], P('gx')
- core_block: float32 [256, 128, 1024], P(('gx', 'gy'), 'gz')
Inputs may be any that keep to these rules, and one draw needn't show every extreme that they name: `volume`: finite entries of order one.
All inputs are finite; a program needn't handle non-finite values.
Results may differ from a plain program's by a relative error of at most 0.0003.
Values sent between devices are 32-bit elements; how exact they have to be, the bound alone decides.
No kernel may reach another device: no remote copies, remote signals or barrier semaphores. Data moves between devices by JAX's collectives and lax.ppermute only.
A program may use at most 64 MiB of HBM per device.

v0:
```python
import jax
import jax.numpy as jnp
from jax import lax
from jax.sharding import PartitionSpec as P

ITERS = 4


def orthonormal(applied):
    highest = lax.Precision.HIGHEST
    products = jnp.dot(applied.T, applied, precision=highest, preferred_element_type=jnp.float32)
    factor_low = jnp.linalg.cholesky(products)
    return lax.linalg.triangular_solve(
        factor_low, applied, left_side=False, lower=True, transpose_a=True
    )


def shards(volume, start_block):
    highest = lax.Precision.HIGHEST
    rows_dev, planes, cols_dev = volume.shape
    flattened = volume.reshape(rows_dev, planes * cols_dev)
    fibres = lax.all_to_all(flattened, "gx", split_axis=1, concat_axis=0, tiled=True)
    scaling = 1.0 / (cols_dev * lax.axis_size("gy") * planes * lax.axis_size("gz"))
    subspace = start_block
    partial_gram = jnp.dot(fibres, fibres.T, precision=highest, preferred_element_type=jnp.float32)
    gram = lax.psum(partial_gram, ("gx", "gy", "gz")) * scaling
    for iteration in range(ITERS):
        applied = jnp.dot(gram, subspace, precision=highest, preferred_element_type=jnp.float32)
        subspace = orthonormal(applied)
    row_offset = lax.axis_index("gx") * rows_dev
    own_rows = lax.dynamic_slice_in_dim(subspace, row_offset, rows_dev, 0)
    core_columns = jnp.dot(
        subspace.T, fibres, precision=highest, preferred_element_type=jnp.float32
    )
    rank_share = lax.all_to_all(core_columns, "gx", split_axis=0, concat_axis=1, tiled=True)
    rank_share = rank_share.reshape(rank_share.shape[0], planes, cols_dev)
    core_block = lax.all_to_all(rank_share, "gy", split_axis=0, concat_axis=2, tiled=True)
    return (own_rows, core_block)


def solution(mesh):
    return jax.shard_map(
        shards,
        mesh=mesh,
        in_specs=(P("gx", "gz", "gy"), P()),
        out_specs=(P("gx", None), P(("gx", "gy"), "gz", None)),
        check_vma=False,
    )
```

profile of v0, /device:TPU:16, one launch (start us, length us, event | category | flops | bytes accessed | tf_op | source)
XLA Modules:
  0.0 684.3 jit_solution(15447810709119931845)
XLA Ops:
  9.1 38.0 %all_to_all.47 = f32[32,32,256]{2,0,1:T(8,128)S(1)} all-to-all(f32[32,32,256]{2,0,1:T(8,128)S(1)} %copy.11), channel_id=1, replica_groups=mesh['gx'=32,'gy'=4,'gz'=4] {'gx'}, dimensions={1} | all-to-all | bytes 2097152 | tf_op jit(solution)/shard_map/all_to_all | solution.py:22
  52.3 285.4 %all-reduce.3.cloned.1.call-done = f32[1024,1024]{1,0:T(8,128)} async-done(((f32[1024,1024]{1,0:T(8,128)}), f32[1024,1024]{1,0:T(8,128)}) %all-reduce.3.cloned.1.call-update) | async-done | bytes 4194320 | tf_op jit(solution)/shard_map/psum | solution.py:26
  337.7 5.4 fusion.6
  347.5 11.7 %cholesky.214 = f32[128,128]{1,0:T(8,128)S(1)} custom-call(f32[128,128]{1,0:T(8,128)S(1)} %cholesky.346), custom_call_target="Cholesky" | custom-call | tf_op jit(solution)/shard_map/jit(cholesky)/cholesky | solution.py:12
  359.3 9.8 %custom-call.17 = f32[1,128,128]{1,2,0:T(8,128)S(1)} custom-call(f32[1,128,128]{2,1,0:T(8,128)S(1)} %get-tuple-element.93), custom_call_target="InvertDiagBlocksLowerTriangular" | custom-call | tf_op jit(solution)/shard_map/jit(cholesky)/cholesky | solution.py:12
  371.3 11.7 %cholesky.231 = f32[128,128]{1,0:T(8,128)S(1)} custom-call(f32[128,128]{1,0:T(8,128)S(1)} %convolution_subtract_fusion.7), custom_call_target="Cholesky" | custom-call | tf_op jit(solution)/shard_map/jit(cholesky)/cholesky | solution.py:12
  391.0 20.5 %custom-call.18 = f32[2,128,128]{1,2,0:T(8,128)S(1)} custom-call(f32[2,128,128]{2,1,0:T(8,128)} %copy-done.11), custom_call_target="InvertDiagBlocksLowerTriangular" | custom-call | tf_op jit(solution)/shard_map/triangular_solve/custom-call.0 | solution.py:13
  413.8 5.3 fusion.4
  423.5 11.7 %cholesky.248 = f32[128,128]{1,0:T(8,128)S(1)} custom-call(f32[128,128]{1,0:T(8,128)S(1)} %cholesky.349), custom_call_target="Cholesky" | custom-call | tf_op jit(solution)/shard_map/jit(cholesky)/cholesky | solution.py:12
  435.3 9.8 %custom-call.19 = f32[1,128,128]{1,2,0:T(8,128)S(1)} custom-call(f32[1,128,128]{2,1,0:T(8,128)S(1)} %get-tuple-element.89), custom_call_target="InvertDiagBlocksLowerTriangular" | custom-call | tf_op jit(solution)/shard_map/jit(cholesky)/cholesky | solution.py:12
  447.3 11.7 %cholesky.265 = f32[128,128]{1,0:T(8,128)S(1)} custom-call(f32[128,128]{1,0:T(8,128)S(1)} %convolution_subtract_fusion.6), custom_call_target="Cholesky" | custom-call | tf_op jit(solution)/shard_map/jit(cholesky)/cholesky | solution.py:12
  467.4 20.5 %custom-call.20 = f32[2,128,128]{1,2,0:T(8,128)S(1)} custom-call(f32[2,128,128]{2,1,0:T(8,128)} %copy-done.12), custom_call_target="InvertDiagBlocksLowerTriangular" | custom-call | tf_op jit(solution)/shard_map/triangular_solve/custom-call.0 | solution.py:13
  490.2 5.7 fusion.2
  500.3 11.7 %cholesky.282 = f32[128,128]{1,0:T(8,128)S(1)} custom-call(f32[128,128]{1,0:T(8,128)S(1)} %cholesky.352), custom_call_target="Cholesky" | custom-call | tf_op jit(solution)/shard_map/jit(cholesky)/cholesky | solution.py:12
  512.1 9.8 %custom-call.21 = f32[1,128,128]{1,2,0:T(8,128)S(1)} custom-call(f32[1,128,128]{2,1,0:T(8,128)S(1)} %get-tuple-element.85), custom_call_target="InvertDiagBlocksLowerTriangular" | custom-call | tf_op jit(solution)/shard_map/jit(cholesky)/cholesky | solution.py:12
  524.1 11.7 %cholesky.299 = f32[128,128]{1,0:T(8,128)S(1)} custom-call(f32[128,128]{1,0:T(8,128)S(1)} %convolution_subtract_fusion.5), custom_call_target="Cholesky" | custom-call | tf_op jit(solution)/shard_map/jit(cholesky)/cholesky | solution.py:12
  544.2 20.5 %custom-call.22 = f32[2,128,128]{1,2,0:T(8,128)S(1)} custom-call(f32[2,128,128]{2,1,0:T(8,128)} %copy-done.13), custom_call_target="InvertDiagBlocksLowerTriangular" | custom-call | tf_op jit(solution)/shard_map/triangular_solve/custom-call.0 | solution.py:13
  567.0 5.3 fusion
  576.7 11.7 %cholesky.316 = f32[128,128]{1,0:T(8,128)S(1)} custom-call(f32[128,128]{1,0:T(8,128)S(1)} %cholesky.355), custom_call_target="Cholesky" | custom-call | tf_op jit(solution)/shard_map/jit(cholesky)/cholesky | solution.py:12
  588.5 9.8 %custom-call.23 = f32[1,128,128]{1,2,0:T(8,128)S(1)} custom-call(f32[1,128,128]{2,1,0:T(8,128)S(1)} %get-tuple-element.81), custom_call_target="InvertDiagBlocksLowerTriangular" | custom-call | tf_op jit(solution)/shard_map/jit(cholesky)/cholesky | solution.py:12
  600.4 11.7 %cholesky.333 = f32[128,128]{1,0:T(8,128)S(1)} custom-call(f32[128,128]{1,0:T(8,128)S(1)} %convolution_subtract_fusion.4), custom_call_target="Cholesky" | custom-call | tf_op jit(solution)/shard_map/jit(cholesky)/cholesky | solution.py:12
  620.8 20.5 %custom-call.24 = f32[2,128,128]{1,2,0:T(8,128)S(1)} custom-call(f32[2,128,128]{2,1,0:T(8,128)} %copy-done.10), custom_call_target="InvertDiagBlocksLowerTriangular" | custom-call | tf_op jit(solution)/shard_map/triangular_solve/custom-call.0 | solution.py:13
  644.6 18.1 %all_to_all.48 = f32[32,8,256]{2,1,0:T(8,128)S(1)} all-to-all(f32[32,8,256]{2,1,0:T(8,128)S(1)} %fusion.13), channel_id=1, replica_groups=mesh['gx'=32,'gy'=4,'gz'=4] {'gx'}, dimensions={0} | all-to-all | bytes 524288 | tf_op jit(solution)/shard_map/all_to_all | solution.py:35
  670.1 6.3 all-to-all-done.2
  (131 shorter events, 95.1 us)
Async XLA Ops:
  7.2 330.5 %copy-start = (f32[1024,256]{1,0:T(8,128)S(1)}, f32[1024,256]{1,0:T(8,128)}, u32[]{:S(2)}) copy-start(f32[1024,256]{1,0:T(8,128)} %param.6) | copy-start | bytes 3145732
  7.2 330.5 %all-reduce.3.cloned.1.call-start = ((), (), s32[]{:S(2)}) async-start(), calls=%async_computation.3 | async-start | bytes 8388608 | tf_op jit(solution)/shard_map/psum | solution.py:26
  346.8 0.7 copy-start.6
  383.0 1.9 copy-start.5
  390.4 0.7 copy-start.11
  422.8 0.7 copy-start.7
  459.0 2.7 copy-start.2
  466.7 0.7 copy-start.12
  499.6 0.7 copy-start.8
  535.8 2.7 copy-start.3
  543.5 0.7 copy-start.13
  576.0 0.7 copy-start.9
  612.2 2.9 copy-start.4
  620.1 0.7 copy-start.10
  641.9 2.7 copy-start.1
  663.4 13.0 %all-to-all-start.2 = ((f32[8,32,256]{2,1,0:T(8,128)}), f32[8,32,256]{2,1,0:T(8,128)S(1)}, u32[]{:S(2)}, u32[]{:S(2)}) async-start(f32[8,32,256]{2,1,0:T(8,128)} %copy.16), calls=%async_computation.2 | async-start | bytes 524288 | tf_op jit(solution)/shard_map/all_to_all | solution.py:37
Sparse Core Ops, SparseCore 0:
  52.4 285.2 all-reduce.2
where the time goes:
time: 690 us; the launch traced here: 684 us
  waiting for transfers between devices  292 us (42%)
  other arithmetic  229 us (33%)
  blocking collectives  56.1 us (8%)
  matrix products  52.9 us (8%)
  local copies, waits for them, and re-layouts  28.8 us (4%)
  between operations  20.4 us (3%)
    psum x1, waiting for transfers between devices, shards(): gram = lax.psum(partial_gram, ('gx', 'gy', 'gz')) * scaling  285 us
    another operation x27, other arithmetic, orthonormal(): factor_low = jnp.linalg.cholesky(products)  138 us
    another operation x10, other arithmetic, orthonormal(): lax.linalg.triangular_solve(factor_low, applied, left_side=False, lower=T...  87.2 us
    all_to_all x1, blocking collectives, shards(): lax.all_to_all(flattened, 'gx', split_axis=1, concat_axis=0, tiled=True)  38 us
    dot_general x4, matrix products, shards(): jnp.dot(gram, subspace, precision=highest, preferred_element_type=jnp.flo...  21.8 us
    all_to_all x1, blocking collectives, shards(): lax.all_to_all(core_columns, 'gx', split_axis=0, concat_axis=1, tiled=True)  18.1 us
    another operation x29, local copies, waits for them, and re-layouts, orthonormal(): lax.linalg.triangular_solve(factor_low, applied, left_side=False, lower=T...  15.9 us
  transfers between devices with their start and end apart: 2, of which 2 were waited for; matrix products, arithmetic and copies ran while one was open for 0% of the time, Pallas kernels for 0%

commit v1 on v0

v1 whole, which is shorter than its diff:
```python
import jax
import jax.numpy as jnp
from jax import lax
from jax.experimental import pallas as pl
from jax.experimental.pallas import tpu as pltpu
from jax.sharding import Mesh, PartitionSpec as P

ITERS = 4
TILE = 128
HIGHEST = lax.Precision.HIGHEST


def triangle(tiles):
    return [(i, j) for i in range(tiles) for j in range(i + 1)]


def gram_kernel(fibres_ref, packed_ref):
    tiles = fibres_ref.shape[0] // TILE
    for pair in range(tiles // 2):
        rows = fibres_ref[pl.ds(2 * TILE * pair, 2 * TILE), :]
        block = lax.dot_general(
            rows,
            fibres_ref[pl.ds(0, 2 * TILE * (pair + 1)), :],
            (((1,), (1,)), ((), ())),
            precision=HIGHEST,
            preferred_element_type=jnp.float32,
        )
        for half in range(2):
            i = 2 * pair + half
            for j in range(i + 1):
                place = (i * (i + 1)) // 2 + j
                packed_ref[pl.ds(place * TILE, TILE), :] = block[
                    half * TILE : (half + 1) * TILE, j * TILE : (j + 1) * TILE
                ]


def packed_gram(fibres):
    rows = fibres.shape[0]
    count = len(triangle(rows // TILE))
    return pl.pallas_call(
        gram_kernel,
        out_shape=jax.ShapeDtypeStruct((count * TILE, TILE), jnp.float32),
        compiler_params=pltpu.CompilerParams(vmem_limit_bytes=32 * 1024 * 1024),
    )(fibres)


def unpack_kernel(scaling, packed_ref, gram_ref):
    tiles = gram_ref.shape[0] // TILE
    for place, (i, j) in enumerate(triangle(tiles)):
        block = packed_ref[pl.ds(place * TILE, TILE), :] * scaling
        gram_ref[pl.ds(i * TILE, TILE), pl.ds(j * TILE, TILE)] = block
        if i != j:
            gram_ref[pl.ds(j * TILE, TILE), pl.ds(i * TILE, TILE)] = block.T


def unpacked_gram(packed, rows, scaling):
    def kernel(packed_ref, gram_ref):
        unpack_kernel(scaling, packed_ref, gram_ref)

    return pl.pallas_call(
        kernel,
        out_shape=jax.ShapeDtypeStruct((rows, rows), jnp.float32),
        compiler_params=pltpu.CompilerParams(vmem_limit_bytes=32 * 1024 * 1024),
    )(packed)


def reduce_scatter(values, axis):
    size = lax.axis_size(axis)
    shares = lax.all_to_all(values, axis, split_axis=0, concat_axis=0, tiled=True)
    return jnp.sum(shares.reshape(size, -1, TILE), axis=0)


def gather(share, axis):
    size = lax.axis_size(axis)
    copies = jnp.broadcast_to(share[None], (size,) + share.shape)
    copies = lax.all_to_all(copies, axis, split_axis=0, concat_axis=0, tiled=True)
    return copies


def sum_over_devices(packed):
    share = packed
    for axis in ("c", "x", "y"):
        share = reduce_scatter(share, axis)
    share = jnp.sum(gather(share, ("zl", "zh")), axis=0)
    for axis in ("y", "x", "c"):
        share = gather(share, axis).reshape(-1, TILE)
    return share


def orthonormal(applied):
    products = jnp.dot(applied.T, applied, precision=HIGHEST, preferred_element_type=jnp.float32)
    factor_low = jnp.linalg.cholesky(products)
    return lax.linalg.triangular_solve(
        factor_low, applied, left_side=False, lower=True, transpose_a=True
    )


def shards(volume, start_block):
    rows_dev, planes, cols_dev = volume.shape
    xy = ("y", "x")
    flattened = volume.reshape(rows_dev, planes * cols_dev)
    fibres = lax.all_to_all(flattened, xy, split_axis=1, concat_axis=0, tiled=True)
    rows = fibres.shape[0]
    scaling = 1.0 / (fibres.shape[1] * lax.axis_size(("y", "x", "zl", "zh", "c")))
    packed = sum_over_devices(packed_gram(fibres))
    gram = unpacked_gram(packed, rows, scaling)
    subspace = start_block
    for iteration in range(ITERS):
        applied = jnp.dot(gram, subspace, precision=HIGHEST, preferred_element_type=jnp.float32)
        subspace = orthonormal(applied)
    row_offset = lax.axis_index(xy) * rows_dev
    own_rows = lax.dynamic_slice_in_dim(subspace, row_offset, rows_dev, 0)
    core_columns = jnp.dot(
        subspace.T, fibres, precision=HIGHEST, preferred_element_type=jnp.float32
    )
    peers = lax.axis_size(("y", "x", "zl"))
    shares = core_columns.reshape(peers, -1, cols_dev)
    shares = lax.all_to_all(shares, ("y", "x", "zl"), split_axis=0, concat_axis=0, tiled=True)
    shares = shares.reshape(planes, -1, shares.shape[1], cols_dev)
    core_block = shares.transpose(2, 0, 1, 3).reshape(shares.shape[2], planes, -1)
    return (own_rows, core_block)


def solution(mesh):
    fine = Mesh(mesh.devices.reshape(8, 4, 4, 2, 2), ("y", "x", "zl", "zh", "c"))
    return jax.shard_map(
        shards,
        mesh=fine,
        in_specs=(P(("y", "x"), ("zh", "c"), "zl"), P()),
        out_specs=(P(("y", "x"), None), P(("y", "x", "zl"), ("zh", "c"), None)),
        check_vma=False,
    )
```

time: 690 us -> 492 us (0.71)
  the two profiles are of different devices: /device:TPU:16 before, /device:TPU:8 now
where the time goes in v1:
time: 492 us; the launch traced here: 486 us
  other arithmetic  233 us (47%)
  blocking collectives  81.9 us (17%)
  waiting for transfers between devices  55 us (11%)
  matrix products  47.6 us (10%)
  local copies, waits for them, and re-layouts  36.2 us (7%)
  starting transfers between devices  22.4 us (5%)
  between operations  7.02 us (1%)
    another operation x27, other arithmetic, orthonormal(): factor_low = jnp.linalg.cholesky(products)  138 us
    another operation x10, other arithmetic, orthonormal(): lax.linalg.triangular_solve(factor_low, applied, left_side=False, lower=T...  86 us
    all_to_all x3, blocking collectives, reduce_scatter(): lax.all_to_all(values, axis, split_axis=0, concat_axis=0, tiled=True)  42.8 us
    all_to_all x3, blocking collectives, gather(): lax.all_to_all(copies, axis, split_axis=0, concat_axis=0, tiled=True)  39.1 us
    all_to_all x1, waiting for transfers between devices, shards(): lax.all_to_all(flattened, xy, split_axis=1, concat_axis=0, tiled=True)  27.3 us
    dot_general x4, matrix products, shards(): jnp.dot(gram, subspace, precision=HIGHEST, preferred_element_type=jnp.flo...  20.2 us
    another operation x29, local copies, waits for them, and re-layouts, orthonormal(): lax.linalg.triangular_solve(factor_low, applied, left_side=False, lower=T...  15.8 us
    all_to_all x1, waiting for transfers between devices, shards(): lax.all_to_all(shares, ('y', 'x', 'zl'), split_axis=0, concat_axis=0, til...  14.5 us
  transfers between devices with their start and end apart: 3, of which 3 were waited for; matrix products, arithmetic and copies ran while one was open for 0% of the time, Pallas kernels for 0%

profile of v1, /device:TPU:8, one launch (start us, length us, event | category | flops | bytes accessed | tf_op | source)
XLA Modules:
  0.0 485.9 jit_solution(8908689427483918378)
XLA Ops:
  3.6 10.2 %all-to-all-start = ((f32[32,32,256]{2,0,1:T(8,128)}), f32[32,32,256]{2,0,1:T(8,128)S(1)}, u32[]{:S(2)}, u32[]{:S(2)}) async-start(f32[32,32,256]{2,0,1:T(8,128)} %copy.20), calls=%async_computation | async-start | bytes 2097152 | tf_op jit(solution)/shard_map/all_to_all | solution.py:102
  13.7 27.3 %all-to-all-done = f32[32,32,256]{2,0,1:T(8,128)S(1)} async-done(((f32[32,32,256]{2,0,1:T(8,128)}), f32[32,32,256]{2,0,1:T(8,128)S(1)}, u32[]{:S(2)}, u32[]{:S(2)}) %all-to-all-start) | async-done | bytes 1048608 | tf_op jit(solution)/shard_map/all_to_all | solution.py:102
  52.8 21.0 %all_to_all.71 = f32[4,576,128]{2,1,0:T(8,128)S(1)} all-to-all(f32[4,576,128]{2,1,0:T(8,128)} %bitcast.168), channel_id=1, replica_groups=mesh['y'=8,'x'=4,'zl'=4,'zh'=2,'c'=2] {'x'}, dimensions={0} | all-to-all | bytes 2359296 | tf_op jit(solution)/shard_map/all_to_all | solution.py:69
  74.5 15.3 %all_to_all.72 = f32[8,72,128]{2,1,0:T(8,128)S(1)} all-to-all(f32[8,72,128]{2,1,0:T(8,128)} %bitcast.169), channel_id=1, replica_groups=mesh['y'=8,'x'=4,'zl'=4,'zh'=2,'c'=2] {'y'}, dimensions={0} | all-to-all | bytes 589824 | tf_op jit(solution)/shard_map/all_to_all | solution.py:69
  89.9 20.0 %all_to_all.73 = f32[8,72,128]{2,1,0:T(8,128)S(1)} all-to-all(f32[8,72,128]{2,1,0:T(8,128)S(1)} %broadcast_in_dim.12), channel_id=1, replica_groups=mesh['y'=8,'x'=4,'zl'=4,'zh'=2,'c'=2] {'zl','zh'}, dimensions={0} | all-to-all | bytes 589824 | tf_op jit(solution)/shard_map/all_to_all | solution.py:76
  110.0 13.5 %all_to_all.69 = f32[8,72,128]{2,1,0:T(8,128)S(1)} all-to-all(f32[8,72,128]{2,1,0:T(8,128)S(1)} %broadcast_in_dim.13), channel_id=1, replica_groups=mesh['y'=8,'x'=4,'zl'=4,'zh'=2,'c'=2] {'y'}, dimensions={0} | all-to-all | bytes 589824 | tf_op jit(solution)/shard_map/all_to_all | solution.py:76
  128.1 13.3 %all-to-all-done.6 = f32[4,576,128]{2,1,0:T(8,128)S(1)} async-done(((f32[4,576,128]{2,1,0:T(8,128)}), f32[4,576,128]{2,1,0:T(8,128)S(1)}, u32[]{:S(2)}, u32[]{:S(2)}) %all-to-all-start.6) | async-done | bytes 1179680 | tf_op jit(solution)/shard_map/all_to_all | solution.py:76
  157.4 11.7 %cholesky.214 = f32[128,128]{1,0:T(8,128)S(1)} custom-call(f32[128,128]{1,0:T(8,128)S(1)} %cholesky.346), custom_call_target="Cholesky" | custom-call | tf_op jit(solution)/shard_map/jit(cholesky)/cholesky | solution.py:92
  169.2 10.0 %custom-call.17 = f32[1,128,128]{1,2,0:T(8,128)S(1)} custom-call(f32[1,128,128]{2,1,0:T(8,128)S(1)} %get-tuple-element.95), custom_call_target="InvertDiagBlocksLowerTriangular" | custom-call | tf_op jit(solution)/shard_map/jit(cholesky)/cholesky | solution.py:92
  181.4 11.7 %cholesky.231 = f32[128,128]{1,0:T(8,128)S(1)} custom-call(f32[128,128]{1,0:T(8,128)S(1)} %convolution_subtract_fusion.7), custom_call_target="Cholesky" | custom-call | tf_op jit(solution)/shard_map/jit(cholesky)/cholesky | solution.py:92
  200.5 20.5 %custom-call.18 = f32[2,128,128]{1,2,0:T(8,128)S(1)} custom-call(f32[2,128,128]{2,1,0:T(8,128)} %copy-done.13), custom_call_target="InvertDiagBlocksLowerTriangular" | custom-call | tf_op jit(solution)/shard_map/triangular_solve/custom-call.0 | solution.py:93
  233.4 11.7 %cholesky.248 = f32[128,128]{1,0:T(8,128)S(1)} custom-call(f32[128,128]{1,0:T(8,128)S(1)} %cholesky.349), custom_call_target="Cholesky" | custom-call | tf_op jit(solution)/shard_map/jit(cholesky)/cholesky | solution.py:92
  245.1 9.8 %custom-call.19 = f32[1,128,128]{1,2,0:T(8,128)S(1)} custom-call(f32[1,128,128]{2,1,0:T(8,128)S(1)} %get-tuple-element.91), custom_call_target="InvertDiagBlocksLowerTriangular" | custom-call | tf_op jit(solution)/shard_map/jit(cholesky)/cholesky | solution.py:92
  257.1 11.7 %cholesky.265 = f32[128,128]{1,0:T(8,128)S(1)} custom-call(f32[128,128]{1,0:T(8,128)S(1)} %convolution_subtract_fusion.6), custom_call_target="Cholesky" | custom-call | tf_op jit(solution)/shard_map/jit(cholesky)/cholesky | solution.py:92
  277.2 20.5 %custom-call.20 = f32[2,128,128]{1,2,0:T(8,128)S(1)} custom-call(f32[2,128,128]{2,1,0:T(8,128)} %copy-done.14), custom_call_target="InvertDiagBlocksLowerTriangular" | custom-call | tf_op jit(solution)/shard_map/triangular_solve/custom-call.0 | solution.py:93
  310.1 11.7 %cholesky.282 = f32[128,128]{1,0:T(8,128)S(1)} custom-call(f32[128,128]{1,0:T(8,128)S(1)} %cholesky.352), custom_call_target="Cholesky" | custom-call | tf_op jit(solution)/shard_map/jit(cholesky)/cholesky | solution.py:92
  321.9 9.8 %custom-call.21 = f32[1,128,128]{1,2,0:T(8,128)S(1)} custom-call(f32[1,128,128]{2,1,0:T(8,128)S(1)} %get-tuple-element.87), custom_call_target="InvertDiagBlocksLowerTriangular" | custom-call | tf_op jit(solution)/shard_map/jit(cholesky)/cholesky | solution.py:92
  333.8 11.7 %cholesky.299 = f32[128,128]{1,0:T(8,128)S(1)} custom-call(f32[128,128]{1,0:T(8,128)S(1)} %convolution_subtract_fusion.5), custom_call_target="Cholesky" | custom-call | tf_op jit(solution)/shard_map/jit(cholesky)/cholesky | solution.py:92
  354.1 20.5 %custom-call.22 = f32[2,128,128]{1,2,0:T(8,128)S(1)} custom-call(f32[2,128,128]{2,1,0:T(8,128)} %copy-done.15), custom_call_target="InvertDiagBlocksLowerTriangular" | custom-call | tf_op jit(solution)/shard_map/triangular_solve/custom-call.0 | solution.py:93
  386.6 11.7 %cholesky.316 = f32[128,128]{1,0:T(8,128)S(1)} custom-call(f32[128,128]{1,0:T(8,128)S(1)} %cholesky.355), custom_call_target="Cholesky" | custom-call | tf_op jit(solution)/shard_map/jit(cholesky)/cholesky | solution.py:92
  398.4 9.8 %custom-call.23 = f32[1,128,128]{1,2,0:T(8,128)S(1)} custom-call(f32[1,128,128]{2,1,0:T(8,128)S(1)} %get-tuple-element.83), custom_call_target="InvertDiagBlocksLowerTriangular" | custom-call | tf_op jit(solution)/shard_map/jit(cholesky)/cholesky | solution.py:92
  410.3 11.7 %cholesky.333 = f32[128,128]{1,0:T(8,128)S(1)} custom-call(f32[128,128]{1,0:T(8,128)S(1)} %convolution_subtract_fusion.4), custom_call_target="Cholesky" | custom-call | tf_op jit(solution)/shard_map/jit(cholesky)/cholesky | solution.py:92
  430.7 20.5 %custom-call.24 = f32[2,128,128]{1,2,0:T(8,128)S(1)} custom-call(f32[2,128,128]{2,1,0:T(8,128)} %copy-done.12), custom_call_target="InvertDiagBlocksLowerTriangular" | custom-call | tf_op jit(solution)/shard_map/triangular_solve/custom-call.0 | solution.py:93
  470.4 14.5 %all-to-all-done.8 = f32[128,2,256]{2,1,0:T(2,128)S(1)} async-done(((f32[128,2,256]{2,1,0:T(2,128)}), f32[128,2,256]{2,1,0:T(2,128)S(1)}, u32[]{:S(2)}, u32[]{:S(2)}) %all-to-all-start.8) | async-done | bytes 262176 | tf_op jit(solution)/shard_map/all_to_all | solution.py:118
  (152 shorter events, 144.6 us)
Async XLA Ops:
  0.6 149.0 %copy-start = (f32[1024,256]{1,0:T(8,128)S(1)}, f32[1024,256]{1,0:T(8,128)}, u32[]{:S(2)}) copy-start(f32[1024,256]{1,0:T(8,128)} %param.6) | copy-start | bytes 3145732
  3.6 37.4 %all-to-all-start = ((f32[32,32,256]{2,0,1:T(8,128)}), f32[32,32,256]{2,0,1:T(8,128)S(1)}, u32[]{:S(2)}, u32[]{:S(2)}) async-start(f32[32,32,256]{2,0,1:T(8,128)} %copy.20), calls=%async_computation | async-start | bytes 2097152 | tf_op jit(solution)/shard_map/all_to_all | solution.py:102
  124.5 16.8 %all-to-all-start.6 = ((f32[4,576,128]{2,1,0:T(8,128)}), f32[4,576,128]{2,1,0:T(8,128)S(1)}, u32[]{:S(2)}, u32[]{:S(2)}) async-start(f32[4,576,128]{2,1,0:T(8,128)} %broadcast_in_dim.30), calls=%async_computation.6 | async-start | bytes 2359296 | tf_op jit(solution)/shard_map/all_to_all | solution.py:76
  147.7 1.9 copy-start.1
  156.7 0.7 copy-start.8
  193.1 1.8 copy-start.7
  199.8 0.7 copy-start.13
  232.6 0.7 copy-start.9
  268.9 2.6 copy-start.4
  276.5 0.7 copy-start.14
  309.4 0.7 copy-start.10
  345.6 2.8 copy-start.5
  353.4 0.7 copy-start.15
  385.9 0.7 copy-start.11
  422.1 2.9 copy-start.6
  430.0 0.7 copy-start.12
  451.8 1.6 copy-start.2
  454.5 15.0 %copy-start.3 = (f32[128,1024]{1,0:T(8,128)S(1)}, f32[128,1024]{1,0:T(8,128)}, u32[]{:S(2)}) copy-start(f32[128,1024]{1,0:T(8,128)} %copy-done.2) | copy-start | bytes 1572868
  460.8 24.0 %all-to-all-start.8 = ((f32[128,2,256]{2,1,0:T(2,128)}), f32[128,2,256]{2,1,0:T(2,128)S(1)}, u32[]{:S(2)}, u32[]{:S(2)}) async-start(f32[128,2,256]{2,1,0:T(2,128)} %copy.26), calls=%async_computation.8 | async-start | bytes 524288 | tf_op jit(solution)/shard_map/all_to_all | solution.py:118

commit v2 on v1

--- a/solution.py
+++ b/solution.py
@@ -7,11 +7,155 @@
 
 ITERS = 4
 TILE = 128
+SUB = 8
+PANEL = 64
 HIGHEST = lax.Precision.HIGHEST
 
 
 def triangle(tiles):
     return [(i, j) for i in range(tiles) for j in range(i + 1)]
+
+
+def unpack(scaling, packed_ref, gram_ref):
+    tiles = gram_ref.shape[0] // TILE
+    for place, (i, j) in enumerate(triangle(tiles)):
+        block = packed_ref[pl.ds(place * TILE, TILE), :] * scaling
+        gram_ref[pl.ds(i * TILE, TILE), pl.ds(j * TILE, TILE)] = block
+        if i != j:
+            gram_ref[pl.ds(j * TILE, TILE), pl.ds(i * TILE, TILE)] = block.T
+
+
+def reciprocal(x):
+    r = pl.reciprocal(x, approx=True)
+    r = r * (2.0 - x * r)
+    return r * (2.0 - x * r)
+
+
+def inverse_root(x):
+    y = lax.rsqrt(x)
+    return y * (1.5 - 0.5 * x * y * y)
+
+
+def along_lanes(x, j):
+    return jnp.broadcast_to(x[:, j : j + 1], (SUB, TILE))
+
+
+def along_sublanes(x, i):
+    return jnp.broadcast_to(x[i : i + 1, :], (SUB, TILE))
+
+
+def factor_panel(work, panel, rec_ref):
+    sub = lax.broadcasted_iota(jnp.int32, (SUB, TILE), 0)
+    lane = lax.broadcasted_iota(jnp.int32, (SUB, TILE), 1)
+    first = panel * PANEL // SUB
+    tiles = list(range(first, first + PANEL // SUB))
+    for k in tiles:
+        home, off = (k * SUB) // TILE, (k * SUB) % TILE
+        inside = (lane >= off) & (lane < off + SUB)
+        cols = {t: [along_lanes(work[t, home], off + j) for j in range(SUB)] for t in tiles if t >= k}
+        unit = jnp.where(lane - off == sub, 1.0, 0.0)
+        for t in tiles:
+            if t == k:
+                work[t, home] = jnp.where(inside, unit, work[t, home])
+            elif t > k:
+                work[t, home] = jnp.where(inside, 0.0, work[t, home])
+        rec = jnp.ones((SUB, TILE), jnp.float32)
+        for j in range(SUB):
+            r = reciprocal(along_sublanes(cols[k][j], j))
+            rec = jnp.where(sub == j, r, rec)
+            upper = [along_sublanes(cols[k][l], j) if l > j else None for l in range(SUB)]
+            row = [along_sublanes(work[k, h], j) for h in range(2)]
+            for t in tiles:
+                if t < k:
+                    continue
+                m = cols[t][j] * r
+                if t == k:
+                    m = jnp.where(sub > j, m, 0.0)
+                for l in range(j + 1, SUB):
+                    cols[t][l] = cols[t][l] - m * upper[l]
+                for h in range(2):
+                    work[t, h] = work[t, h] - m * row[h]
+        rec_ref[pl.ds(k * SUB, SUB), :] = rec
+
+
+def inverse_factor(prod_ref, rec_ref):
+    order = prod_ref.shape[0]
+    halves = order // TILE
+    for panel in range(order // PANEL):
+        start = panel * PANEL
+        work = {}
+        for t in range(start // SUB, (start + PANEL) // SUB):
+            for h in range(halves):
+                work[t, h] = prod_ref[pl.ds(t * SUB, SUB), pl.ds(h * TILE, TILE)]
+        factor_panel(work, panel, rec_ref)
+        for (t, h), value in work.items():
+            prod_ref[pl.ds(t * SUB, SUB), pl.ds(h * TILE, TILE)] = value
+        rest = order - start - PANEL
+        if rest:
+            rows = prod_ref[pl.ds(start, PANEL), :]
+            rec = rec_ref[pl.ds(start, PANEL), :]
+            low = (start + PANEL) // TILE * TILE
+            scaled = jnp.concatenate([rows[:, h * TILE : (h + 1) * TILE] * rec for h in range(low // TILE, halves)], axis=1)
+            r_io = lax.broadcasted_iota(jnp.int32, rows.shape, 0) + start
+            c_io = lax.broadcasted_iota(jnp.int32, rows.shape, 1)
+            lower = jnp.where((c_io > r_io) & (c_io < start + PANEL), 0.0, rows)
+            update = lax.dot_general(scaled, lower, (((0,), (0,)), ((), ())), precision=HIGHEST, preferred_element_type=jnp.float32)
+            update = update[start + PANEL - low :, :]
+            old = prod_ref[pl.ds(start + PANEL, rest), :]
+            c_io = lax.broadcasted_iota(jnp.int32, old.shape, 1)
+            old = jnp.where((c_io >= start) & (c_io < start + PANEL), 0.0, old)
+            prod_ref[pl.ds(start + PANEL, rest), :] = old - update
+    root = inverse_root(rec_ref[...])
+    root = rec_ref[...] * root
+    r_io = lax.broadcasted_iota(jnp.int32, (order, TILE), 0)
+    for h in range(halves):
+        c_io = lax.broadcasted_iota(jnp.int32, (order, TILE), 1) + h * TILE
+        value = prod_ref[:, pl.ds(h * TILE, TILE)]
+        prod_ref[:, pl.ds(h * TILE, TILE)] = jnp.where(c_io <= r_io, value * root, 0.0)
+
+
+def iterate_kernel(scaling, own_ref, packed_ref, start_ref, fibres_ref, rows_ref, core_ref, gram_ref, sub_ref, app_ref, prod_ref, rec_ref):
+    unpack(scaling, packed_ref, gram_ref)
+    sub_ref[...] = start_ref[...]
+    chunk = 256
+    chunks = gram_ref.shape[0] // chunk
+
+    @pl.loop(0, ITERS)
+    def _(step):
+        prod_ref[...] = jnp.zeros_like(prod_ref)
+
+        @pl.loop(0, chunks)
+        def _(i):
+            part = jnp.dot(gram_ref[pl.ds(i * chunk, chunk), :], sub_ref[...], precision=HIGHEST, preferred_element_type=jnp.float32)
+            app_ref[pl.ds(i * chunk, chunk), :] = part
+            prod_ref[...] += lax.dot_general(part, part, (((0,), (0,)), ((), ())), precision=HIGHEST, preferred_element_type=jnp.float32)
+
+        inverse_factor(prod_ref, rec_ref)
+
+        @pl.loop(0, chunks)
+        def _(i):
+            sub_ref[pl.ds(i * chunk, chunk), :] = lax.dot_general(
+                app_ref[pl.ds(i * chunk, chunk), :], prod_ref[...], (((1,), (1,)), ((), ())), precision=HIGHEST, preferred_element_type=jnp.float32)
+
+    own = rows_ref.shape[0]
+    rows_ref[...] = sub_ref[pl.ds(pl.multiple_of(own_ref[0] * own, own), own), :]
+    core_ref[...] = lax.dot_general(sub_ref[...], fibres_ref[...], (((0,), (0,)), ((), ())), precision=HIGHEST, preferred_element_type=jnp.float32)
+
+
+def iterate(packed, start, fibres, own, own_rows, scaling):
+    rows, rank = start.shape
+    def kernel(*refs):
+        iterate_kernel(scaling, *refs)
+    vmem = pl.BlockSpec(memory_space=pltpu.VMEM)
+    return pl.pallas_call(
+        kernel,
+        out_shape=(jax.ShapeDtypeStruct((own_rows, rank), jnp.float32), jax.ShapeDtypeStruct((rank, fibres.shape[1]), jnp.float32)),
+        in_specs=[pl.BlockSpec(memory_space=pltpu.SMEM), vmem, vmem, vmem],
+        out_specs=(vmem, vmem),
+        scratch_shapes=[pltpu.VMEM((rows, rows), jnp.float32), pltpu.VMEM((rows, rank), jnp.float32), pltpu.VMEM((rows, rank), jnp.float32),
+                        pltpu.VMEM((rank, rank), jnp.float32), pltpu.VMEM((rank, TILE), jnp.float32)],
+        compiler_params=pltpu.CompilerParams(vmem_limit_bytes=48 * 1024 * 1024),
+    )(own, packed, start, fibres)
 
 
 def gram_kernel(fibres_ref, packed_ref):
@@ -44,26 +188,6 @@
     )(fibres)
 
 
-def unpack_kernel(scaling, packed_ref, gram_ref):
-    tiles = gram_ref.shape[0] // TILE
-    for place, (i, j) in enumerate(triangle(tiles)):
-        block = packed_ref[pl.ds(place * TILE, TILE), :] * scaling
-        gram_ref[pl.ds(i * TILE, TILE), pl.ds(j * TILE, TILE)] = block
-        if i != j:
-            gram_ref[pl.ds(j * TILE, TILE), pl.ds(i * TILE, TILE)] = block.T
-
-
-def unpacked_gram(packed, rows, scaling):
-    def kernel(packed_ref, gram_ref):
-        unpack_kernel(scaling, packed_ref, gram_ref)
-
-    return pl.pallas_call(
-        kernel,
-        out_shape=jax.ShapeDtypeStruct((rows, rows), jnp.float32),
-        compiler_params=pltpu.CompilerParams(vmem_limit_bytes=32 * 1024 * 1024),
-    )(packed)
-
-
 def reduce_scatter(values, axis):
     size = lax.axis_size(axis)
     shares = lax.all_to_all(values, axis, split_axis=0, concat_axis=0, tiled=True)
@@ -87,31 +211,15 @@
     return share
 
 
-def orthonormal(applied):
-    products = jnp.dot(applied.T, applied, precision=HIGHEST, preferred_element_type=jnp.float32)
-    factor_low = jnp.linalg.cholesky(products)
-    return lax.linalg.triangular_solve(
-        factor_low, applied, left_side=False, lower=True, transpose_a=True
-    )
-
-
 def shards(volume, start_block):
     rows_dev, planes, cols_dev = volume.shape
     xy = ("y", "x")
     flattened = volume.reshape(rows_dev, planes * cols_dev)
     fibres = lax.all_to_all(flattened, xy, split_axis=1, concat_axis=0, tiled=True)
-    rows = fibres.shape[0]
     scaling = 1.0 / (fibres.shape[1] * lax.axis_size(("y", "x", "zl", "zh", "c")))
     packed = sum_over_devices(packed_gram(fibres))
-    gram = unpacked_gram(packed, rows, scaling)
-    subspace = start_block
-    for iteration in range(ITERS):
-        applied = jnp.dot(gram, subspace, precision=HIGHEST, preferred_element_type=jnp.float32)
-        subspace = orthonormal(applied)
-    row_offset = lax.axis_index(xy) * rows_dev
-    own_rows = lax.dynamic_slice_in_dim(subspace, row_offset, rows_dev, 0)
-    core_columns = jnp.dot(
-        subspace.T, fibres, precision=HIGHEST, preferred_element_type=jnp.float32
+    own_rows, core_columns = iterate(
+        packed, start_block, fibres, lax.axis_index(xy).reshape(1), rows_dev, scaling
     )
     peers = lax.axis_size(("y", "x", "zl"))
     shares = core_columns.reshape(peers, -1, cols_dev)

time: 492 us -> 247 us (0.50); the launches traced: 486 us -> 247 us
  other arithmetic: 233 us -> 1.39 us
  Pallas kernels: 2.84 us -> 81.6 us
  blocking collectives: 81.9 us -> 142 us
  matrix products: 47.6 us -> 0 us
  waiting for transfers between devices: 55 us -> 13.2 us
  local copies, waits for them, and re-layouts: 36.2 us -> 4.18 us
  starting transfers between devices: 22.4 us -> 3.53 us
  between operations: 7.02 us -> 0.71 us
    another operation x37 -> x0, other arithmetic: 224 us -> none  [the longest x27 138 us: orthonormal(): factor_low = jnp.linalg.cholesky(products)]
    pallas_call x1, Pallas kernels: 0.57 us -> 79.3 us  [iterate(): pl.pallas_call(kernel, out_shape=(jax.ShapeDtypeStruct((own_rows, rank),...]
    all_to_all x0 -> x2, blocking collectives: none -> 61 us  [the longest x1 37.2 us: shards(): lax.all_to_all(flattened, xy, split_axis=1, concat_axis=0, tiled=True)]
    all_to_all x2 -> x0, waiting for transfers between devices: 41.7 us -> none  [the longest x1 27.3 us: shards(): lax.all_to_all(flattened, xy, split_axis=1, concat_axis=0, tiled=True)]
    dot_general x9 -> x0, matrix products: 30 us -> none  [the longest x4 20.2 us: shards(): jnp.dot(gram, subspace, precision=HIGHEST, preferred_element_type=jnp.flo...]
    all_to_all x2 -> x0, starting transfers between devices: 18.9 us -> none  [the longest x1 10.2 us: shards(): lax.all_to_all(flattened, xy, split_axis=1, concat_axis=0, tiled=True)]
    another operation x20 -> x0, matrix products: 17.7 us -> none  [the longest x12 9.04 us: orthonormal(): lax.linalg.triangular_solve(factor_low, applied, left_side=False, lower=T...]
    another operation x37 -> x0, local copies, waits for them, and re-layouts: 15.9 us -> none  [the longest x29 15.8 us: orthonormal(): lax.linalg.triangular_solve(factor_low, applied, left_side=False, lower=T...]
  transfers between devices with their start and end apart: 3 -> 1, of which waited for: 3 -> 1; matrix products, arithmetic and copies ran while one was open for 0% -> 0% of each run, Pallas kernels for 0% -> 0%
where the time goes in v2:
time: 247 us
  blocking collectives  142 us (57%)
  Pallas kernels  81.6 us (33%)
  waiting for transfers between devices  13.2 us (5%)
  local copies, waits for them, and re-layouts  4.18 us (2%)
  starting transfers between devices  3.53 us (1%)
    pallas_call x1, Pallas kernels, iterate(): pl.pallas_call(kernel, out_shape=(jax.ShapeDtypeStruct((own_rows, rank),...  79.3 us
    all_to_all x3, blocking collectives, reduce_scatter(): lax.all_to_all(values, axis, split_axis=0, concat_axis=0, tiled=True)  41.7 us
    all_to_all x3, blocking collectives, gather(): lax.all_to_all(copies, axis, split_axis=0, concat_axis=0, tiled=True)  39.2 us
    all_to_all x1, blocking collectives, shards(): lax.all_to_all(flattened, xy, split_axis=1, concat_axis=0, tiled=True)  37.2 us
    all_to_all x1, blocking collectives, shards(): lax.all_to_all(shares, ('y', 'x', 'zl'), split_axis=0, concat_axis=0, til...  23.7 us
    all_to_all x1, waiting for transfers between devices, gather(): lax.all_to_all(copies, axis, split_axis=0, concat_axis=0, tiled=True)  13.2 us
  transfers between devices with their start and end apart: 1, of which 1 were waited for; matrix products, arithmetic and copies ran while one was open for 0% of the time, Pallas kernels for 0%

profile of v2, /device:TPU:8, one launch (start us, length us, event | category | flops | bytes accessed | tf_op | source)
XLA Modules:
  0.0 246.5 jit_solution(14670321936250279876)
XLA Ops:
  0.6 1.8 copy.8
  2.5 37.2 %all_to_all.68 = f32[32,32,256]{2,0,1:T(8,128)S(1)} all-to-all(f32[32,32,256]{2,0,1:T(8,128)S(1)} %copy.8), channel_id=1, replica_groups=mesh['y'=8,'x'=4,'zl'=4,'zh'=2,'c'=2] {'y','x'}, dimensions={1} | all-to-all | bytes 2097152 | tf_op jit(solution)/shard_map/all_to_all | solution.py:218
  39.7 2.3 shard_map.41
  42.0 5.6 %all_to_all.69 = f32[2,2304,128]{2,1,0:T(8,128)S(1)} all-to-all(f32[2,2304,128]{2,1,0:T(8,128)S(1)} %bitcast.17), channel_id=1, replica_groups=mesh['y'=8,'x'=4,'zl'=4,'zh'=2,'c'=2] {'c'}, dimensions={0} | all-to-all | bytes 4718592 | tf_op jit(solution)/shard_map/all_to_all | solution.py:193
  47.6 1.3 reduce_sum.36
  48.9 21.0 %all_to_all.70 = f32[4,576,128]{2,1,0:T(8,128)S(1)} all-to-all(f32[4,576,128]{2,1,0:T(8,128)} %bitcast.19), channel_id=1, replica_groups=mesh['y'=8,'x'=4,'zl'=4,'zh'=2,'c'=2] {'x'}, dimensions={0} | all-to-all | bytes 2359296 | tf_op jit(solution)/shard_map/all_to_all | solution.py:193
  69.8 0.1 reduce_sum.37
  69.9 15.1 %all_to_all.71 = f32[8,72,128]{2,1,0:T(8,128)S(1)} all-to-all(f32[8,72,128]{2,1,0:T(8,128)S(1)} %bitcast.20), channel_id=1, replica_groups=mesh['y'=8,'x'=4,'zl'=4,'zh'=2,'c'=2] {'y'}, dimensions={0} | all-to-all | bytes 589824 | tf_op jit(solution)/shard_map/all_to_all | solution.py:193
  85.1 20.0 %all_to_all.72 = f32[8,72,128]{2,1,0:T(8,128)S(1)} all-to-all(f32[8,72,128]{2,1,0:T(8,128)S(1)} %broadcast_in_dim.12), channel_id=1, replica_groups=mesh['y'=8,'x'=4,'zl'=4,'zh'=2,'c'=2] {'zl','zh'}, dimensions={0} | all-to-all | bytes 589824 | tf_op jit(solution)/shard_map/all_to_all | solution.py:200
  105.2 13.4 %all_to_all.73 = f32[8,72,128]{2,1,0:T(8,128)S(1)} all-to-all(f32[8,72,128]{2,1,0:T(8,128)S(1)} %broadcast_in_dim.13), channel_id=1, replica_groups=mesh['y'=8,'x'=4,'zl'=4,'zh'=2,'c'=2] {'y'}, dimensions={0} | all-to-all | bytes 589824 | tf_op jit(solution)/shard_map/all_to_all | solution.py:200
  118.6 1.1 broadcast_in_dim.29
  119.7 3.5 %all-to-all-start.6 = ((f32[4,576,128]{2,1,0:T(8,128)}), f32[4,576,128]{2,1,0:T(8,128)S(1)}, u32[]{:S(2)}, u32[]{:S(2)}) async-start(f32[4,576,128]{2,1,0:T(8,128)} %broadcast_in_dim.29), calls=%async_computation.6 | async-start | bytes 2359296 | tf_op jit(solution)/shard_map/all_to_all | solution.py:200
  123.2 13.2 %all-to-all-done.6 = f32[4,576,128]{2,1,0:T(8,128)S(1)} async-done(((f32[4,576,128]{2,1,0:T(8,128)}), f32[4,576,128]{2,1,0:T(8,128)S(1)}, u32[]{:S(2)}, u32[]{:S(2)}) %all-to-all-start.6) | async-done | bytes 1179680 | tf_op jit(solution)/shard_map/all_to_all | solution.py:200
  136.5 0.2 broadcast_in_dim.31
  136.6 0.0 copy-start
  136.6 5.8 %all_to_all.74 = f32[2,2304,128]{2,1,0:T(8,128)S(1)} all-to-all(f32[2,2304,128]{2,1,0:T(8,128)S(1)} %broadcast_in_dim.31), channel_id=1, replica_groups=mesh['y'=8,'x'=4,'zl'=4,'zh'=2,'c'=2] {'c'}, dimensions={0} | all-to-all | bytes 4718592 | tf_op jit(solution)/shard_map/all_to_all | solution.py:200
  142.4 0.0 copy-done
  142.4 79.3 %shard_map.42 = (f32[32,256]{1,0:T(8,128)}, f32[256,256]{1,0:T(8,128)S(1)}) custom-call(s32[1]{0:T(128)} %bitcast.refs_0_, f32[4608,128]{1,0:T(8,128)S(1)} %bitcast.16, f32[1024,256]{1,0:T(8,128)S(1)} %copy-done, f32[1024,256]{1,0:T(8,128)S(1)} %bitcast.15), custom_call_target="tpu_custom_call" | custom-call | tf_op jit(solution)/shard_map/pallas_call | solution.py:150
  221.7 0.1 reshape.42
  221.9 23.7 %all_to_all.75 = f32[128,2,256]{2,1,0:T(2,128)S(1)} all-to-all(f32[128,2,256]{2,1,0:T(2,128)S(1)} %reshape.42), channel_id=1, replica_groups=mesh['y'=8,'x'=4,'zl'=4,'zh'=2,'c'=2] {'y','x','zl'}, dimensions={0} | all-to-all | bytes 524288 | tf_op jit(solution)/shard_map/all_to_all | solution.py:226
  245.6 0.1 copy.11
  245.7 0.8 reshape.44
  (4 shorter events, 0.1 us)
Async XLA Ops:
  119.7 16.8 %all-to-all-start.6 = ((f32[4,576,128]{2,1,0:T(8,128)}), f32[4,576,128]{2,1,0:T(8,128)S(1)}, u32[]{:S(2)}, u32[]{:S(2)}) async-start(f32[4,576,128]{2,1,0:T(8,128)} %broadcast_in_dim.29), calls=%async_computation.6 | async-start | bytes 2359296 | tf_op jit(solution)/shard_map/all_to_all | solution.py:200
  136.6 5.8 %copy-start = (f32[1024,256]{1,0:T(8,128)S(1)}, f32[1024,256]{1,0:T(8,128)}, u32[]{:S(2)}) copy-start(f32[1024,256]{1,0:T(8,128)} %refs_2_.1) | copy-start | bytes 3145732
